TPU v7x, 32 devices: a whole 2x2x4 slice. The times are simulated.
32 devices in a mesh: grp: 4 (over y, core), dev: 8 (over z, x).
Axes of the slice: x: 2, y: 2, z: 4, core: 2. Of those that a mesh axis runs over, the one named last changes fastest.
Arguments:
- points: bfloat16 [12288, 128], P(('grp', 'dev')), may hold values from -6 to 6
- start_vectors: float32 [12288, 32], P(('grp', 'dev')), may hold values from -6 to 6
Outputs:
- embedding: float32 [12288, 32], P(('grp', 'dev'))
All inputs are finite; a program needn't handle non-finite values.
Results may differ from a plain program's by a relative error of at most 0.005.
Values may be sent and summed in bfloat16 or wider, within the bound.
A program may use at most 128 MiB of HBM per device.

v0:
```python
import math
import jax
import jax.numpy as jnp
from jax import lax
from jax.sharding import PartitionSpec as P

ITERS = 2
sharpness = 8.0
panels_per_block = 16


def unit_rows(points):
    values = points.astype(jnp.float32)
    squares = jnp.sum(values * values, axis=-1, keepdims=True)
    return (values * lax.rsqrt(squares + 1e-06)).astype(jnp.bfloat16)


def tile_weights(own_units, others):
    cosine = lax.dot_general(
        own_units, others, (((1,), (1,)), ((), ())), preferred_element_type=jnp.float32
    )
    return jnp.exp(sharpness * (cosine - 1.0)).astype(jnp.bfloat16)


def weight_panel(own_units, rolled, count):
    tile_rows = own_units.shape[0]
    width = panels_per_block * tile_rows

    def fill(index, panel):
        others = lax.dynamic_slice_in_dim(rolled, index * width, width, 0)
        return lax.dynamic_update_slice_in_dim(
            panel, tile_weights(own_units, others), index * width, 1
        )

    empty = jnp.zeros((tile_rows, count * tile_rows), jnp.bfloat16)
    return lax.fori_loop(0, count // panels_per_block, fill, empty)


def share_iterate(iterate):
    return lax.all_gather(iterate, ("grp", "dev"), axis=0, tiled=True)


def orthonormal(image):
    gram_local = jnp.dot(
        image.T, image, precision=lax.Precision.HIGHEST, preferred_element_type=jnp.float32
    )
    gram_total = lax.psum(gram_local, ("grp", "dev"))
    factor = jnp.linalg.cholesky(gram_total)
    return lax.linalg.triangular_solve(factor, image.T, left_side=True, lower=True).T


def body(points, start_vectors):
    tile_rows = points.shape[0]
    panels = lax.axis_size(("grp", "dev"))
    position = lax.axis_index(("grp", "dev"))
    own_units = unit_rows(points)
    all_units = lax.all_gather(own_units, ("grp", "dev"), axis=0, tiled=True)
    rolled = jnp.roll(all_units, -position * tile_rows, axis=0)
    vectors = start_vectors
    weights = weight_panel(own_units, rolled, panels)
    degree = jnp.sum(weights, axis=1, dtype=jnp.float32)
    scale = lax.rsqrt(degree)[:, None]
    for sweep in range(ITERS):
        iterate = (scale * vectors).astype(jnp.bfloat16)
        gathered = jnp.roll(share_iterate(iterate), -position * tile_rows, axis=0)
        product = jnp.dot(weights, gathered, preferred_element_type=jnp.float32)
        vectors = orthonormal(scale * product)
    return vectors * math.sqrt(tile_rows * panels)


def solution(mesh):
    placed = (P(("grp", "dev"), None), P(("grp", "dev"), None))
    return jax.shard_map(
        body, mesh=mesh, in_specs=placed, out_specs=P(("grp", "dev"), None), check_vma=False
    )
```

profile of v0, /device:TPU:14, one launch (start us, length us, event | category | flops | bytes accessed | tf_op | source)
XLA Modules:
  0.0 340.0 jit_solution(12517805892950426013)
XLA Ops:
  6.5 1.0 fusion.12
  7.6 1.7 fusion.13
  9.3 59.4 %all-gather.2.cloned.1.call-done = bf16[12288,128]{1,0:T(8,128)(2,1)} async-done(((bf16[384,128]{1,0:T(8,128)(2,1)}), bf16[12288,128]{1,0:T(8,128)(2,1)}) %all-gather.2.cloned.1.call-update) | async-done | bytes 3145744 | tf_op jit(solution)/shard_map/all_gather | solution.py:57
  68.6 4.2 %fusion.4 = bf16[12288,128]{1,0:T(8,128)(2,1)S(1)} fusion(s32[]{:T(128)S(6)} %select_n.35, bf16[12288,128]{1,0:T(8,128)(2,1)} %all-gather.2.cloned.1.call-done), kind=kLoop, calls=%fused_computation.8 | loop fusion | flops 6291456 | bytes 6291460 | tf_op jit(solution)/shard_map/jit(_roll_dynamic)/concatenate | solution.py:58
  72.9 4.4 %broadcast_in_dim.2 = bf16[384,12288]{0,1:T(8,128)(2,1)} broadcast(bf16[]{:T(256)} %constant.130.clone.1), dimensions={} | broadcast | bytes 9437186 | tf_op jit(solution)/shard_map/broadcast_in_dim | solution.py:35
  77.3 7.7 %while.15 = (s32[]{:T(128)}, bf16[384,12288]{0,1:T(8,128)(2,1)}, bf16[12288,128]{1,0:T(8,128)(2,1)S(1)}, bf16[384,128]{1,0:T(8,128)(2,1)S(1)}, s32[]{:T(128)}, /*index=5*/s32[]{:T(128)}, s32[]{:T(128)}, s32[]{:T(128)}) while((s32[]{:T(128)}, bf16[384,12288]{0,1:T(8,128)(2,1)}, bf16[12288,128]{1,0:T(8,128)(2,1)S(1)}, ...), condition=%wide.region_2.3_spmd, body=%wide.region_1.2_spmd.sunk | while | flops 611057664 | bytes 6390915 | solution.py:36
  77.3 3.8 %fusion.42 = bf16[384,12288]{0,1:T(8,128)(2,1)} fusion(bf16[384,12288]{0,1:T(8,128)(2,1)} %get-tuple-element.161, s32[]{:T(128)S(6)} %select_n.52, bf16[384,128]{1,0:T(8,128)(2,1)S(1)} %get-tuple-element.171, bf16[12288,128]{1,0:T(8,128)(2,1)S(1)} %get-tuple-element.170), kind=kOutput, calls=%fused_computation.2.clone.1 | convolution fusion | flops 611057664 | bytes 6390784 | tf_op jit(solution)/shard_map/while/body/eval_jaxpr/dot_general | solution.py:19
  81.1 3.9 %fusion.42 = bf16[384,12288]{0,1:T(8,128)(2,1)} fusion(bf16[384,12288]{0,1:T(8,128)(2,1)} %get-tuple-element.161, s32[]{:T(128)S(6)} %select_n.52, bf16[384,128]{1,0:T(8,128)(2,1)S(1)} %get-tuple-element.171, bf16[12288,128]{1,0:T(8,128)(2,1)S(1)} %get-tuple-element.170), kind=kOutput, calls=%fused_computation.2.clone.1 | convolution fusion | flops 611057664 | bytes 6390784 | tf_op jit(solution)/shard_map/while/body/eval_jaxpr/dot_general | solution.py:19
  85.0 6.4 %convert_reduce_fusion = f32[384]{0:T(512)S(1)} fusion(bf16[384,12288]{0,1:T(8,128)(2,1)} %get-tuple-element.118), kind=kLoop, calls=%fused_computation.5 | loop fusion | flops 9436800 | bytes 9438720 | tf_op jit(solution)/shard_map/reduce_sum | solution.py:61
  91.5 68.2 %all_gather.10 = bf16[12288,32]{0,1:T(8,128)(2,1)S(1)} all-gather(bf16[384,32]{0,1:T(8,128)(2,1)S(1)} %multiply_convert_fusion), channel_id=1, replica_groups=mesh['grp'=4,'dev'=8] {'grp','dev'}, dimensions={0}, use_global_device_ids=true | all-gather | bytes 811008 | tf_op jit(solution)/shard_map/all_gather | solution.py:40
  159.7 1.7 convolution_multiply_fusion.1
  161.6 43.7 %psum.14 = f32[32,32]{0,1:T(8,128)S(1)} all-reduce(f32[32,32]{0,1:T(8,128)S(1)} %fusion.28), channel_id=1, replica_groups=mesh['grp'=4,'dev'=8] {'grp','dev'}, use_global_device_ids=true, to_apply=%region_4.6 | all-reduce | flops 1024 | bytes 8192 | tf_op jit(solution)/shard_map/psum | solution.py:47
  205.4 2.9 cholesky.44
  208.3 0.6 compare_reduce_fusion.1
  209.0 0.7 fusion.16
  209.6 2.4 custom-call.6
  212.3 64.6 %all_gather.11 = bf16[12288,32]{0,1:T(8,128)(2,1)S(1)} all-gather(bf16[384,32]{0,1:T(8,128)(2,1)S(1)} %fusion.7), channel_id=1, replica_groups=mesh['grp'=4,'dev'=8] {'grp','dev'}, dimensions={0}, use_global_device_ids=true | all-gather | bytes 811008 | tf_op jit(solution)/shard_map/all_gather | solution.py:40
  276.9 5.4 %convolution_multiply_fusion = f32[384,32]{0,1:T(8,128)S(1)} fusion(bf16[384,12288]{0,1:T(8,128)(2,1)} %get-tuple-element.118, s32[]{:T(128)S(6)} %select_n.35, bf16[12288,32]{0,1:T(8,128)(2,1)S(1)} %all_gather.11, f32[384]{0:T(512)S(1)} %rsqrt.16), kind=kOutput, calls=%fused_computation.13 | convolution fusion | flops 303575040 | bytes 10274308 | tf_op jit(solution)/shard_map/dot_general | solution.py:66
  282.5 43.0 %psum.15 = f32[32,32]{0,1:T(8,128)S(1)} all-reduce(f32[32,32]{0,1:T(8,128)S(1)} %fusion.29), channel_id=1, replica_groups=mesh['grp'=4,'dev'=8] {'grp','dev'}, use_global_device_ids=true, to_apply=%region_7.11 | all-reduce | flops 1024 | bytes 8192 | tf_op jit(solution)/shard_map/psum | solution.py:47
  325.6 2.9 cholesky.55
  328.5 0.6 compare_reduce_fusion
  329.2 0.7 fusion.17
  329.8 2.4 custom-call.7
  332.3 0.9 fusion.5
  (20 shorter events, 0.9 us)
Async XLA Ops:
  6.5 62.1 %all-gather.2.cloned.1.call-start = ((), (), s32[]{:S(2)}) async-start(), calls=%async_computation | async-start | bytes 3244032 | tf_op jit(solution)/shard_map/all_gather | solution.py:57
  72.9 4.4 %copy-start.1 = (bf16[384,128]{1,0:T(8,128)(2,1)S(1)}, bf16[384,128]{1,0:T(8,128)(2,1)}, u32[]{:S(2)}) copy-start(bf16[384,128]{1,0:T(8,128)(2,1)} %fusion.13) | copy-start | bytes 294916
  77.3 14.1 %copy-start.2 = (f32[384,32]{0,1:T(8,128)S(1)}, f32[384,32]{0,1:T(8,128)}, u32[]{:S(2)}) copy-start(f32[384,32]{0,1:T(8,128)} %param.10) | copy-start | bytes 147460
  85.0 74.7 %copy-start = (bf16[384,12288]{0,1:T(8,128)(2,1)S(1)}, bf16[384,12288]{0,1:T(8,128)(2,1)}, u32[]{:S(2)}) copy-start(bf16[384,12288]{0,1:T(8,128)(2,1)} %get-tuple-element.118) | copy-start | bytes 28311556
Sparse Core Ops, SparseCore 0:
  10.3 58.2 all-gather.1
where the time goes:
time: 341 us; the launch traced here: 340 us
  blocking collectives  219 us (64%)
  waiting for transfers between devices  59.4 us (17%)
  other arithmetic  26.7 us (8%)
  matrix products  16.3 us (5%)
  between operations  13.5 us (4%)
  local copies, waits for them, and re-layouts  4.56 us (1%)
    all_gather x2, blocking collectives, share_iterate(): return lax.all_gather(iterate, ('grp', 'dev'), axis=0, tiled=True)  133 us
    psum x2, blocking collectives, orthonormal(): gram_total = lax.psum(gram_local, ('grp', 'dev'))  86.7 us
    all_gather x1, waiting for transfers between devices, body(): all_units = lax.all_gather(own_units, ('grp', 'dev'), axis=0, tiled=True)  59.4 us
    dot_general x2, matrix products, tile_weights(): lax.dot_general(own_units, others, (((1,), (1,)), ((), ())), preferred_el...  7.69 us
    another operation x6, other arithmetic, orthonormal(): factor = jnp.linalg.cholesky(gram_total)  7.19 us
    dot_general x2, matrix products, body(): product = jnp.dot(weights, gathered, preferred_element_type=jnp.float32)  7.09 us
  transfers between devices with their start and end apart: 1, of which 1 were waited for; matrix products, arithmetic and copies ran while one was open for 0% of the time, Pallas kernels for 0%

commit v1 on v0

--- a/solution.py
+++ b/solution.py
@@ -44,7 +44,7 @@
     gram_local = jnp.dot(
         image.T, image, precision=lax.Precision.HIGHEST, preferred_element_type=jnp.float32
     )
-    gram_total = lax.psum(gram_local, ("grp", "dev"))
+    gram_total = jnp.sum(lax.all_gather(gram_local, ("grp", "dev")), axis=0)
     factor = jnp.linalg.cholesky(gram_total)
     return lax.linalg.triangular_solve(factor, image.T, left_side=True, lower=True).T
 

time: 341 us -> 398 us (1.17)
  blocking collectives: 219 us -> 274 us
    all_gather x0 -> x2, blocking collectives: none -> 138 us  [orthonormal(): gram_total = jnp.sum(lax.all_gather(gram_local, ('grp', 'dev')), axis=0)]
    psum x2 -> x0, blocking collectives: 86.7 us -> none  [orthonormal(): gram_total = lax.psum(gram_local, ('grp', 'dev'))]
where the time goes in v1:
time: 398 us; the launch traced here: 395 us
  blocking collectives  274 us (69%)
  waiting for transfers between devices  59.4 us (15%)
  other arithmetic  26.8 us (7%)
  matrix products  16.3 us (4%)
  between operations  13.5 us (3%)
  local copies, waits for them, and re-layouts  4.56 us (1%)
    all_gather x2, blocking collectives, orthonormal(): gram_total = jnp.sum(lax.all_gather(gram_local, ('grp', 'dev')), axis=0)  138 us
    all_gather x2, blocking collectives, share_iterate(): return lax.all_gather(iterate, ('grp', 'dev'), axis=0, tiled=True)  136 us
    all_gather x1, waiting for transfers between devices, body(): all_units = lax.all_gather(own_units, ('grp', 'dev'), axis=0, tiled=True)  59.4 us
  transfers between devices with their start and end apart: 1, of which 1 were waited for; matrix products, arithmetic and copies ran while one was open for 0% of the time, Pallas kernels for 0%

profile of v1, /device:TPU:14, one launch (start us, length us, event | category | flops | bytes accessed | tf_op | source)
XLA Modules:
  0.0 394.8 jit_solution(2802606807349853417)
XLA Ops:
  6.5 1.0 fusion.12
  7.6 1.7 fusion.13
  9.3 59.4 %all-gather.4.cloned.1.call-done = bf16[12288,128]{1,0:T(8,128)(2,1)} async-done(((bf16[384,128]{1,0:T(8,128)(2,1)}), bf16[12288,128]{1,0:T(8,128)(2,1)}) %all-gather.4.cloned.1.call-update) | async-done | bytes 3145744 | tf_op jit(solution)/shard_map/all_gather | solution.py:57
  68.6 4.2 %fusion.4 = bf16[12288,128]{1,0:T(8,128)(2,1)S(1)} fusion(s32[]{:T(128)S(6)} %select_n.35, bf16[12288,128]{1,0:T(8,128)(2,1)} %all-gather.4.cloned.1.call-done), kind=kLoop, calls=%fused_computation.8 | loop fusion | flops 6291456 | bytes 6291460 | tf_op jit(solution)/shard_map/jit(_roll_dynamic)/concatenate | solution.py:58
  72.9 4.4 %broadcast_in_dim.2 = bf16[384,12288]{0,1:T(8,128)(2,1)} broadcast(bf16[]{:T(256)} %constant.130.clone.1), dimensions={} | broadcast | bytes 9437186 | tf_op jit(solution)/shard_map/broadcast_in_dim | solution.py:35
  77.3 7.7 %while.15 = (s32[]{:T(128)}, bf16[384,12288]{0,1:T(8,128)(2,1)}, bf16[12288,128]{1,0:T(8,128)(2,1)S(1)}, bf16[384,128]{1,0:T(8,128)(2,1)S(1)}, s32[]{:T(128)}, /*index=5*/s32[]{:T(128)}, s32[]{:T(128)}, s32[]{:T(128)}) while((s32[]{:T(128)}, bf16[384,12288]{0,1:T(8,128)(2,1)}, bf16[12288,128]{1,0:T(8,128)(2,1)S(1)}, ...), condition=%wide.region_2.3_spmd, body=%wide.region_1.2_spmd.sunk | while | flops 611057664 | bytes 6390915 | solution.py:36
  77.3 3.8 fusion.42
  81.1 3.9 fusion.42
  85.0 6.4 %convert_reduce_fusion = f32[384]{0:T(512)S(1)} fusion(bf16[384,12288]{0,1:T(8,128)(2,1)} %get-tuple-element.118), kind=kLoop, calls=%fused_computation.5 | loop fusion | flops 9436800 | bytes 9438720 | tf_op jit(solution)/shard_map/reduce_sum | solution.py:61
  91.5 68.2 %all_gather.22 = bf16[12288,32]{0,1:T(8,128)(2,1)S(1)} all-gather(bf16[384,32]{0,1:T(8,128)(2,1)S(1)} %multiply_convert_fusion), channel_id=1, replica_groups=mesh['grp'=4,'dev'=8] {'grp','dev'}, dimensions={0}, use_global_device_ids=true | all-gather | bytes 811008 | tf_op jit(solution)/shard_map/all_gather | solution.py:40
  159.7 1.7 convolution_multiply_fusion.1
  161.6 69.1 %all-gather = f32[1024,32]{1,0:T(8,128)S(1)} all-gather(f32[32,32]{1,0:T(8,128)S(1)} %fusion.28), channel_id=2, replica_groups=mesh['grp'=4,'dev'=8] {'grp','dev'}, dimensions={0}, use_global_device_ids=true | all-gather | bytes 135168 | tf_op jit(solution)/shard_map/all_gather | solution.py:47
  230.8 2.9 cholesky.44
  233.8 0.6 compare_reduce_fusion.1
  234.4 0.7 fusion.16
  235.1 2.4 custom-call.6
  237.8 67.9 %all_gather.25 = bf16[12288,32]{0,1:T(8,128)(2,1)S(1)} all-gather(bf16[384,32]{0,1:T(8,128)(2,1)S(1)} %fusion.7), channel_id=1, replica_groups=mesh['grp'=4,'dev'=8] {'grp','dev'}, dimensions={0}, use_global_device_ids=true | all-gather | bytes 811008 | tf_op jit(solution)/shard_map/all_gather | solution.py:40
  305.7 5.4 %convolution_multiply_fusion = f32[384,32]{0,1:T(8,128)S(1)} fusion(bf16[384,12288]{0,1:T(8,128)(2,1)} %get-tuple-element.118, s32[]{:T(128)S(6)} %select_n.35, bf16[12288,32]{0,1:T(8,128)(2,1)S(1)} %all_gather.25, f32[384]{0:T(512)S(1)} %rsqrt.16), kind=kOutput, calls=%fused_computation.13 | convolution fusion | flops 303575040 | bytes 10274308 | tf_op jit(solution)/shard_map/dot_general | solution.py:66
  311.2 69.0 %all-gather.1 = f32[1024,32]{1,0:T(8,128)S(1)} all-gather(f32[32,32]{1,0:T(8,128)S(1)} %fusion.29), channel_id=3, replica_groups=mesh['grp'=4,'dev'=8] {'grp','dev'}, dimensions={0}, use_global_device_ids=true | all-gather | bytes 135168 | tf_op jit(solution)/shard_map/all_gather | solution.py:47
  380.4 2.9 cholesky.55
  383.4 0.6 compare_reduce_fusion
  384.0 0.7 fusion.17
  384.7 2.4 custom-call.7
  387.1 0.9 fusion.5
  (22 shorter events, 1.0 us)
Async XLA Ops:
  6.5 62.1 %all-gather.4.cloned.1.call-start = ((), (), s32[]{:S(2)}) async-start(), calls=%async_computation | async-start | bytes 3244032 | tf_op jit(solution)/shard_map/all_gather | solution.py:57
  72.9 4.4 %copy-start.1 = (bf16[384,128]{1,0:T(8,128)(2,1)S(1)}, bf16[384,128]{1,0:T(8,128)(2,1)}, u32[]{:S(2)}) copy-start(bf16[384,128]{1,0:T(8,128)(2,1)} %fusion.13) | copy-start | bytes 294916
  77.3 14.1 %copy-start.2 = (f32[384,32]{0,1:T(8,128)S(1)}, f32[384,32]{0,1:T(8,128)}, u32[]{:S(2)}) copy-start(f32[384,32]{0,1:T(8,128)} %param.10) | copy-start | bytes 147460
  85.0 74.7 %copy-start = (bf16[384,12288]{0,1:T(8,128)(2,1)S(1)}, bf16[384,12288]{0,1:T(8,128)(2,1)}, u32[]{:S(2)}) copy-start(bf16[384,12288]{0,1:T(8,128)(2,1)} %get-tuple-element.118) | copy-start | bytes 28311556
Sparse Core Ops, SparseCore 0:
  10.3 58.2 all-gather.3

commit v2 on v0

--- a/solution.py
+++ b/solution.py
@@ -44,7 +44,7 @@
     gram_local = jnp.dot(
         image.T, image, precision=lax.Precision.HIGHEST, preferred_element_type=jnp.float32
     )
-    gram_total = lax.psum(gram_local, ("grp", "dev"))
+    gram_total = lax.psum(lax.psum(gram_local, "dev"), "grp")
     factor = jnp.linalg.cholesky(gram_total)
     return lax.linalg.triangular_solve(factor, image.T, left_side=True, lower=True).T
 

time: 341 us -> 351 us (1.029)
  the two profiles are of different devices: /device:TPU:14 before, /device:TPU:0 now
where the time goes in v2:
time: 351 us
  blocking collectives  227 us (65%)
  waiting for transfers between devices  62.9 us (18%)
  other arithmetic  26.8 us (8%)
  matrix products  16.3 us (5%)
  between operations  13.5 us (4%)
  local copies, waits for them, and re-layouts  4.56 us (1%)
    all_gather x2, blocking collectives, share_iterate(): return lax.all_gather(iterate, ('grp', 'dev'), axis=0, tiled=True)  139 us
    psum x4, blocking collectives, orthonormal(): gram_total = lax.psum(lax.psum(gram_local, 'dev'), 'grp')  87.8 us
    all_gather x1, waiting for transfers between devices, body(): all_units = lax.all_gather(own_units, ('grp', 'dev'), axis=0, tiled=True)  62.8 us
    dot_general x2, matrix products, tile_weights(): lax.dot_general(own_units, others, (((1,), (1,)), ((), ())), preferred_el...  7.7 us
    another operation x6, other arithmetic, orthonormal(): factor = jnp.linalg.cholesky(gram_total)  7.19 us
    dot_general x2, matrix products, body(): product = jnp.dot(weights, gathered, preferred_element_type=jnp.float32)  7.1 us
  transfers between devices with their start and end apart: 1, of which 1 were waited for; matrix products, arithmetic and copies ran while one was open for 0% of the time, Pallas kernels for 0%

profile of v2, /device:TPU:0, one launch (start us, length us, event | category | flops | bytes accessed | tf_op | source)
XLA Modules:
  0.0 350.9 jit_solution(7912149055157934587)
XLA Ops:
  6.5 1.0 fusion.12
  7.6 1.7 fusion.13
  9.3 62.8 %all-gather.2.cloned.1.call-done = bf16[12288,128]{1,0:T(8,128)(2,1)} async-done(((bf16[384,128]{1,0:T(8,128)(2,1)}), bf16[12288,128]{1,0:T(8,128)(2,1)}) %all-gather.2.cloned.1.call-update) | async-done | bytes 3145744 | tf_op jit(solution)/shard_map/all_gather | solution.py:57
  72.1 4.3 %fusion.4 = bf16[12288,128]{1,0:T(8,128)(2,1)S(1)} fusion(s32[]{:T(128)S(6)} %select_n.35, bf16[12288,128]{1,0:T(8,128)(2,1)} %all-gather.2.cloned.1.call-done), kind=kLoop, calls=%fused_computation.8 | loop fusion | flops 6291456 | bytes 6291460 | tf_op jit(solution)/shard_map/jit(_roll_dynamic)/concatenate | solution.py:58
  76.4 4.4 %broadcast_in_dim.2 = bf16[384,12288]{0,1:T(8,128)(2,1)} broadcast(bf16[]{:T(256)} %constant.130.clone.1), dimensions={} | broadcast | bytes 9437186 | tf_op jit(solution)/shard_map/broadcast_in_dim | solution.py:35
  80.8 7.7 %while.15 = (s32[]{:T(128)}, bf16[384,12288]{0,1:T(8,128)(2,1)}, bf16[12288,128]{1,0:T(8,128)(2,1)S(1)}, bf16[384,128]{1,0:T(8,128)(2,1)S(1)}, s32[]{:T(128)}, /*index=5*/s32[]{:T(128)}, s32[]{:T(128)}, s32[]{:T(128)}) while((s32[]{:T(128)}, bf16[384,12288]{0,1:T(8,128)(2,1)}, bf16[12288,128]{1,0:T(8,128)(2,1)S(1)}, ...), condition=%wide.region_2.3_spmd, body=%wide.region_1.2_spmd.sunk | while | flops 611057664 | bytes 6390915 | solution.py:36
  80.8 3.8 %fusion.42 = bf16[384,12288]{0,1:T(8,128)(2,1)} fusion(bf16[384,12288]{0,1:T(8,128)(2,1)} %get-tuple-element.161, s32[]{:T(128)S(6)} %select_n.52, bf16[384,128]{1,0:T(8,128)(2,1)S(1)} %get-tuple-element.171, bf16[12288,128]{1,0:T(8,128)(2,1)S(1)} %get-tuple-element.170), kind=kOutput, calls=%fused_computation.2.clone.1 | convolution fusion | flops 611057664 | bytes 6390784 | tf_op jit(solution)/shard_map/while/body/eval_jaxpr/dot_general | solution.py:19
  84.7 3.9 %fusion.42 = bf16[384,12288]{0,1:T(8,128)(2,1)} fusion(bf16[384,12288]{0,1:T(8,128)(2,1)} %get-tuple-element.161, s32[]{:T(128)S(6)} %select_n.52, bf16[384,128]{1,0:T(8,128)(2,1)S(1)} %get-tuple-element.171, bf16[12288,128]{1,0:T(8,128)(2,1)S(1)} %get-tuple-element.170), kind=kOutput, calls=%fused_computation.2.clone.1 | convolution fusion | flops 611057664 | bytes 6390784 | tf_op jit(solution)/shard_map/while/body/eval_jaxpr/dot_general | solution.py:19
  88.5 6.4 %convert_reduce_fusion = f32[384]{0:T(512)S(1)} fusion(bf16[384,12288]{0,1:T(8,128)(2,1)} %get-tuple-element.118), kind=kLoop, calls=%fused_computation.5 | loop fusion | flops 9436800 | bytes 9438720 | tf_op jit(solution)/shard_map/reduce_sum | solution.py:61
  95.0 70.7 %all_gather.10 = bf16[12288,32]{0,1:T(8,128)(2,1)S(1)} all-gather(bf16[384,32]{0,1:T(8,128)(2,1)S(1)} %multiply_convert_fusion), channel_id=1, replica_groups=mesh['grp'=4,'dev'=8] {'grp','dev'}, dimensions={0}, use_global_device_ids=true | all-gather | bytes 811008 | tf_op jit(solution)/shard_map/all_gather | solution.py:40
  165.7 1.7 convolution_multiply_fusion.1
  167.6 33.0 %psum.28 = f32[32,32]{0,1:T(8,128)S(1)} all-reduce(f32[32,32]{0,1:T(8,128)S(1)} %fusion.28), channel_id=1, replica_groups=mesh['grp'=4,'dev'=8] {'dev'}, use_global_device_ids=true, to_apply=%region_4.6 | all-reduce | flops 1024 | bytes 8192 | tf_op jit(solution)/shard_map/psum | solution.py:47
  200.6 10.1 %psum.29 = f32[32,32]{0,1:T(8,128)S(1)} all-reduce(f32[32,32]{0,1:T(8,128)S(1)} %psum.28), channel_id=1, replica_groups=mesh['grp'=4,'dev'=8] {'grp'}, use_global_device_ids=true, to_apply=%region_5.7 | all-reduce | flops 1024 | bytes 8192 | tf_op jit(solution)/shard_map/psum | solution.py:47
  210.8 2.9 cholesky.44
  214.4 0.7 fusion.16
  215.1 2.4 custom-call.6
  217.8 68.4 %all_gather.11 = bf16[12288,32]{0,1:T(8,128)(2,1)S(1)} all-gather(bf16[384,32]{0,1:T(8,128)(2,1)S(1)} %fusion.7), channel_id=1, replica_groups=mesh['grp'=4,'dev'=8] {'grp','dev'}, dimensions={0}, use_global_device_ids=true | all-gather | bytes 811008 | tf_op jit(solution)/shard_map/all_gather | solution.py:40
  286.1 5.4 %convolution_multiply_fusion = f32[384,32]{0,1:T(8,128)S(1)} fusion(bf16[384,12288]{0,1:T(8,128)(2,1)} %get-tuple-element.118, s32[]{:T(128)S(6)} %select_n.35, bf16[12288,32]{0,1:T(8,128)(2,1)S(1)} %all_gather.11, f32[384]{0:T(512)S(1)} %rsqrt.16), kind=kOutput, calls=%fused_computation.13 | convolution fusion | flops 303575040 | bytes 10274308 | tf_op jit(solution)/shard_map/dot_general | solution.py:66
  291.7 34.6 %psum.30 = f32[32,32]{0,1:T(8,128)S(1)} all-reduce(f32[32,32]{0,1:T(8,128)S(1)} %fusion.29), channel_id=1, replica_groups=mesh['grp'=4,'dev'=8] {'dev'}, use_global_device_ids=true, to_apply=%region_8.12 | all-reduce | flops 1024 | bytes 8192 | tf_op jit(solution)/shard_map/psum | solution.py:47
  326.3 10.1 %psum.31 = f32[32,32]{0,1:T(8,128)S(1)} all-reduce(f32[32,32]{0,1:T(8,128)S(1)} %psum.30), channel_id=1, replica_groups=mesh['grp'=4,'dev'=8] {'grp'}, use_global_device_ids=true, to_apply=%region_9.13 | all-reduce | flops 1024 | bytes 8192 | tf_op jit(solution)/shard_map/psum | solution.py:47
  336.5 2.9 cholesky.55
  340.1 0.7 fusion.17
  340.7 2.4 custom-call.7
  343.2 0.9 fusion.5
  (22 shorter events, 2.2 us)
Async XLA Ops:
  6.5 65.6 %all-gather.2.cloned.1.call-start = ((), (), s32[]{:S(2)}) async-start(), calls=%async_computation | async-start | bytes 3244032 | tf_op jit(solution)/shard_map/all_gather | solution.py:57
  76.4 4.4 %copy-start.1 = (bf16[384,128]{1,0:T(8,128)(2,1)S(1)}, bf16[384,128]{1,0:T(8,128)(2,1)}, u32[]{:S(2)}) copy-start(bf16[384,128]{1,0:T(8,128)(2,1)} %fusion.13) | copy-start | bytes 294916
  80.8 14.1 %copy-start.2 = (f32[384,32]{0,1:T(8,128)S(1)}, f32[384,32]{0,1:T(8,128)}, u32[]{:S(2)}) copy-start(f32[384,32]{0,1:T(8,128)} %param.10) | copy-start | bytes 147460
  88.5 77.1 %copy-start = (bf16[384,12288]{0,1:T(8,128)(2,1)S(1)}, bf16[384,12288]{0,1:T(8,128)(2,1)}, u32[]{:S(2)}) copy-start(bf16[384,12288]{0,1:T(8,128)(2,1)} %get-tuple-element.118) | copy-start | bytes 28311556
Sparse Core Ops, SparseCore 0:
  10.3 61.7 all-gather.1
